TPU v7x, 32 devices: a whole 2x2x4 slice. The times are simulated.
32 devices in a mesh: parts: 2 (over y), rep: 4 (over x, core), tp: 4 (over z).
Axes of the slice: x: 2, y: 2, z: 4, core: 2. Of those that a mesh axis runs over, the one named last changes fastest.
Arguments:
- gate_inputs: bfloat16 [6, 128, 8192], P(None, ('parts', 'rep'), 'tp'), parts along dimension 1, may hold values from -12 to 12
- conv_inputs: bfloat16 [6, 128, 8192], P(None, ('parts', 'rep'), 'tp'), parts along dimension 1, may hold values from -6 to 6
- bc_inputs: bfloat16 [6, 128, 2048], P(None, ('parts', 'rep')), parts along dimension 1, may hold values from -6 to 6
- delta_inputs: bfloat16 [6, 128, 128], P(None, ('parts', 'rep'), 'tp'), parts along dimension 1, may hold values from -5 to 5
- conv_weight: float32 [4, 8192], P(None, 'tp'), may hold values from -3 to 3
- conv_bias: float32 [8192], P('tp'), may hold values from -3 to 3
- bc_weight: float32 [4, 2048], replicated, may hold values from -3 to 3
- bc_bias: float32 [2048], replicated, may hold values from -3 to 3
- delta_bias: float32 [128], P('tp'), may hold values from -2 to 0.5
- decay_rate: float32 [128], P('tp'), may hold values from 0.02 to 3
- skip_gain: float32 [128], P('tp'), may hold values from 1 to 4
- norm_gain: float32 [8192], P('tp'), may hold values from 0.1 to 1.9
- out_weight: bfloat16 [8192, 4096], P('tp'), may hold values from -0.09375 to 0.09375
- ssd_state: float32 [128, 128, 64, 128], P(('parts', 'rep'), 'tp'), parts along dimension 0, may hold values from -3 to 3
- conv_state: bfloat16 [128, 3, 8192], P(('parts', 'rep'), None, 'tp'), parts along dimension 0, may hold values from -6 to 6
- bc_state: bfloat16 [128, 3, 2048], P(('parts', 'rep')), parts along dimension 0, may hold values from -6 to 6
- finish_step: int32 [128], P(('parts', 'rep')), parts along dimension 0, may hold values from 1 to 12, as said below
- move_plan: int32 [2, 4, 4, 2, 2], P('parts'), parts along dimension 0, may hold values from -1 to 15, as said below
Outputs:
- layer_out: bfloat16 [6, 128, 4096], P(None, ('parts', 'rep'), 'tp'), parts along dimension 1
There are 2 independent parts, one for each index of `parts`. A program takes and returns all parts, laid end to end along the dimension named above; an argument that names none is the same for every part. Nothing has to cross between parts.
Inputs may be any that keep to these rules, and one draw needn't show every extreme that they name: A slot emits outputs at steps t < finish_step. `move_plan`: entry [k, i, j, c] is (source slot on replica i, destination slot on replica j) or (-1, -1) when unused; no entry has i == j; within one k, the used source slots of one replica are distinct and the used destination slots of one replica are distinct; at every migration some pair (i, j) uses all 2 lanes and some replica receives 2 rollouts from every other replica.
All inputs are finite; a program needn't handle non-finite values.
Results may differ from a plain program's by a relative error of at most 0.005.
Values may be sent and summed in bfloat16 or wider, within the bound.
A program may use at most 192 MiB of HBM per device.

v0:
```python
import jax
import jax.numpy as jnp
from jax import lax
from jax.sharding import PartitionSpec as P

HEADS = 128
HEAD_DIM = 64
STATE = 128
GROUPS = 8
PERIOD = 3
MIGR = 1
INNER = 8192


norm_eps = 1e-05


def body(
    gate_inputs,
    conv_inputs,
    bc_inputs,
    delta_inputs,
    conv_weight,
    conv_bias,
    bc_weight,
    bc_bias,
    delta_bias,
    decay_rate,
    skip_gain,
    norm_gain,
    out_weight,
    ssd_state,
    conv_state,
    bc_state,
    finish_step,
    move_plan,
):
    slot_count = finish_step.shape[0]
    heads_here = delta_inputs.shape[2]
    inner_here = gate_inputs.shape[2]
    per_group = HEADS // GROUPS
    replica = lax.axis_index("rep")
    head_ids = lax.axis_index("tp") * heads_here + jnp.arange(heads_here, dtype=jnp.int32)
    selector = (
        head_ids[:, None] // per_group == jnp.arange(GROUPS, dtype=jnp.int32)[None, :]
    ).astype(jnp.float32)

    def project(hidden):
        return lax.psum_scatter(
            lax.dot_general(
                out_weight, hidden, (((0,), (1,)), ((), ())), preferred_element_type=jnp.float32
            ),
            "tp",
            scatter_dimension=0,
            tiled=True,
        ).T

    def advance(carried, inputs):
        states, stored, stored_bc, life_ends = carried
        gate_step, conv_step, bc_step, delta_step, step_id = inputs
        is_live = step_id < life_ends
        window = jnp.concatenate([stored, conv_step[:, None, :]], axis=1)
        mixed_conv = jnp.sum(window.astype(jnp.float32) * conv_weight[None], axis=1) + conv_bias
        stored = jnp.where(is_live[:, None, None], window[:, 1:], stored)
        bc_window = jnp.concatenate([stored_bc, bc_step[:, None, :]], axis=1)
        mixed_bc = jnp.sum(bc_window.astype(jnp.float32) * bc_weight[None], axis=1) + bc_bias
        stored_bc = jnp.where(is_live[:, None, None], bc_window[:, 1:], stored_bc)
        x_heads = jax.nn.silu(mixed_conv).reshape(slot_count, heads_here, HEAD_DIM)
        bc_act = jax.nn.silu(mixed_bc).reshape(slot_count, GROUPS, 2, STATE)
        b_heads = jnp.einsum(
            "sgn,hg->shn", bc_act[:, :, 0], selector, precision=lax.Precision.HIGHEST
        )
        c_heads = jnp.einsum(
            "sgn,hg->shn", bc_act[:, :, 1], selector, precision=lax.Precision.HIGHEST
        )
        step_size = jax.nn.softplus(delta_step.astype(jnp.float32) + delta_bias)
        retained = jnp.exp(-step_size * decay_rate)
        updated = (
            retained[:, :, None, None] * states
            + (step_size[:, :, None] * x_heads)[:, :, :, None] * b_heads[:, :, None, :]
        )
        states = jnp.where(is_live[:, None, None, None], updated, states)
        head_out = jnp.einsum("shpn,shn->shp", states, c_heads, precision=lax.Precision.HIGHEST)
        head_out = head_out + skip_gain[None, :, None] * x_heads
        gated = (
            head_out
            * jax.nn.silu(gate_step.astype(jnp.float32)).reshape(slot_count, heads_here, HEAD_DIM)
        ).reshape(slot_count, inner_here)
        local_squares = jnp.sum(gated * gated, axis=1)
        sum_total = lax.psum(local_squares, "tp")
        inv_rms = lax.rsqrt(sum_total / INNER + norm_eps)
        hidden = (gated * inv_rms[:, None] * norm_gain).astype(jnp.bfloat16)
        projected = project(hidden)
        row_scale = is_live.astype(jnp.float32)
        return (
            (states, stored, stored_bc, life_ends),
            (projected * row_scale[:, None]).astype(jnp.bfloat16),
        )

    carried = (ssd_state, conv_state, bc_state, finish_step)
    pieces = []
    for period in range(MIGR + 1):
        if period > 0:
            migrate_states = carried[0]
            migrate_stored = carried[1]
            migrate_stored_bc = carried[2]
            migrate_life_ends = carried[3]
            layer_plan = move_plan[period - 1]
            outbound = layer_plan[replica]
            sources = outbound[..., 0]
            is_used = sources >= 0
            migrate_picked = jnp.where(is_used, sources, 0)
            sent_states = migrate_states[migrate_picked]
            sent_rows = migrate_stored[migrate_picked].astype(jnp.float32)
            sent_bc = migrate_stored_bc[migrate_picked].astype(jnp.float32)
            sent_ends = jnp.where(is_used, migrate_life_ends[migrate_picked], 0).astype(jnp.float32)
            recv_states = lax.all_to_all(
                sent_states.astype(jnp.bfloat16), "rep", split_axis=0, concat_axis=0, tiled=True
            ).astype(sent_states.dtype)
            recv_rows = lax.all_to_all(
                sent_rows.astype(jnp.bfloat16), "rep", split_axis=0, concat_axis=0, tiled=True
            ).astype(sent_rows.dtype)
            recv_bc = lax.all_to_all(
                sent_bc.astype(jnp.bfloat16), "rep", split_axis=0, concat_axis=0, tiled=True
            ).astype(sent_bc.dtype)
            recv_ends = lax.all_to_all(
                sent_ends.astype(jnp.bfloat16), "rep", split_axis=0, concat_axis=0, tiled=True
            ).astype(sent_ends.dtype)
            inbound = jnp.take(layer_plan, replica, axis=1)[..., 1]
            target = jnp.where(inbound >= 0, inbound, slot_count).reshape(-1)
            cleared = jnp.where(is_used, sources, slot_count).reshape(-1)
            migrate_life_ends = migrate_life_ends.at[cleared].set(0, mode="drop")
            migrate_life_ends = migrate_life_ends.at[target].set(
                recv_ends.reshape(-1).astype(jnp.int32), mode="drop"
            )
            migrate_states = migrate_states.at[target].set(
                recv_states.reshape((-1,) + migrate_states.shape[1:]), mode="drop"
            )
            migrate_stored = migrate_stored.at[target].set(
                recv_rows.reshape((-1,) + migrate_stored.shape[1:]).astype(jnp.bfloat16),
                mode="drop",
            )
            migrate_stored_bc = migrate_stored_bc.at[target].set(
                recv_bc.reshape((-1,) + migrate_stored_bc.shape[1:]).astype(jnp.bfloat16),
                mode="drop",
            )
            carried = (migrate_states, migrate_stored, migrate_stored_bc, migrate_life_ends)
        first = period * PERIOD
        final = first + PERIOD
        step_ids = jnp.arange(first, final, dtype=jnp.int32)
        carried, mixed_rows = lax.scan(
            advance,
            carried,
            (
                gate_inputs[first:final],
                conv_inputs[first:final],
                bc_inputs[first:final],
                delta_inputs[first:final],
                step_ids,
            ),
        )
        pieces.append(mixed_rows)
    return jnp.concatenate(pieces, axis=0)


def solution(mesh):
    in_specs = (
        P(None, ("parts", "rep"), "tp"),
        P(None, ("parts", "rep"), "tp"),
        P(None, ("parts", "rep"), None),
        P(None, ("parts", "rep"), "tp"),
        P(None, "tp"),
        P("tp"),
        P(),
        P(),
        P("tp"),
        P("tp"),
        P("tp"),
        P("tp"),
        P("tp", None),
        P(("parts", "rep"), "tp", None, None),
        P(("parts", "rep"), None, "tp"),
        P(("parts", "rep"), None, None),
        P(("parts", "rep")),
        P("parts", None, None, None, None),
    )
    out_specs = P(None, ("parts", "rep"), "tp")
    return jax.shard_map(body, mesh=mesh, in_specs=in_specs, out_specs=out_specs, check_vma=False)
```

profile of v0, /device:TPU:0, one launch (start us, length us, event | category | flops | bytes accessed | tf_op | source)
XLA Modules:
  0.0 629.8 jit_solution(87304279674689172)
XLA Ops:
  7.3 11.9 %copy.155 = f32[16,32,64,128]{3,2,1,0:T(8,128)} copy(f32[16,32,64,128]{3,2,1,0:T(8,128)} %param.35) | data formatting | bytes 33554432
  20.9 4.2 all-to-all-start.3
  25.4 250.9 %while.35 = (s32[]{:T(128)}, f32[16,32,64,128]{3,2,1,0:T(8,128)}, bf16[16,3,2048]{2,0,1:T(8,128)(2,1)S(1)}, bf16[16,3,2048]{2,0,1:T(8,128)(2,1)S(1)}, bf16[3,16,...) while((s32[]{:T(128)}, f32[16,32,64,128]{3,2,1,0:T(8,128)}, ...), condition=%wide.region_6.7_spmd.clone, body=%wide.region_0.6_spmd.clone.sunk | while | flops 350492736 | bytes 75214536 | solution.py:151
  28.4 13.0 %add_select_fusion.4 = f32[16,32,64,128]{3,2,1,0:T(8,128)} fusion(f32[16,32,64,128]{3,2,1,0:T(8,128)} %get-tuple-element.761, f32[16,32,128]{2,1,0:T(8,128)S(1)} %convolution_bitcast_fusion.8, f32[16,32,64]{2,1,0:T(8,128)S(1)} %broadcast_multiply_fusion.4, f32[16,32]{1,0:T(8,128)S(1)} %get-tuple-element.700, pred[16]{0:T(512)(128)(4,1)S(1)} %get-tuple-element.701), kind=kLoop, calls=%fused_computation.11.clone.1 | loop fusion | flops 16777216 | bytes 33949712 | tf_op jit(solution)/shard_map/while/body/eval_jaxpr/jit(_where)/select_n | solution.py:82
  41.4 28.6 %fusion.91 = f32[16,32,1,64]{3,2,1,0:T(1,128)S(1)} fusion(f32[16,32,64,128]{3,2,1,0:T(8,128)} %add_select_fusion.4, f32[16,32,128,1]{2,3,1,0:T(1,128)S(1)} %bitcast.175), kind=kOutput, calls=%fused_computation.138.clone.1 | convolution fusion | flops 50331648 | bytes 17170432 | tf_op jit(solution)/shard_map/while/body/eval_jaxpr/shpn,shn->shp/dot_general | solution.py:83
  70.5 12.4 %psum.18 = f32[16]{0:T(128)S(1)} all-reduce(f32[16]{0:T(128)S(1)} %get-tuple-element.705), channel_id=1, replica_groups=mesh['parts'=2,'rep'=4,'tp'=4] {'tp'}, use_global_device_ids=true, to_apply=%region_4.4 | all-reduce | flops 16 | bytes 128 | tf_op jit(solution)/shard_map/while/body/eval_jaxpr/psum | solution.py:90
  82.9 8.8 %convolution_bitcast_fusion.9 = f32[4096,16]{0,1:T(8,128)} fusion(bf16[2048,4096]{1,0:T(8,128)(2,1)} %get-tuple-element.801, f32[16,2048]{1,0:T(8,128)S(1)} %reshape.530, f32[2048]{0:T(1024)S(1)} %get-tuple-element.800, f32[16]{0:T(128)S(1)} %add_rsqrt_fusion.4), kind=kOutput, calls=%fused_computation.12.clone.1 | convolution fusion | flops 268533760 | bytes 17178688 | tf_op jit(solution)/shard_map/while/body/eval_jaxpr/dot_general | solution.py:50
  91.8 18.4 %reduce-scatter.3.cloned.1.call-done = f32[1024,16]{0,1:T(8,128)} async-done(((f32[4096,16]{0,1:T(8,128)}), f32[1024,16]{0,1:T(8,128)}) %reduce-scatter.3.cloned.1.call-update) | async-done | bytes 65552 | tf_op jit(solution)/shard_map/while/body/eval_jaxpr/reduce_scatter | solution.py:49
  114.0 13.0 %add_select_fusion.4 = f32[16,32,64,128]{3,2,1,0:T(8,128)} fusion(f32[16,32,64,128]{3,2,1,0:T(8,128)} %get-tuple-element.761, f32[16,32,128]{2,1,0:T(8,128)S(1)} %convolution_bitcast_fusion.8, f32[16,32,64]{2,1,0:T(8,128)S(1)} %broadcast_multiply_fusion.4, f32[16,32]{1,0:T(8,128)S(1)} %get-tuple-element.700, pred[16]{0:T(512)(128)(4,1)S(1)} %get-tuple-element.701), kind=kLoop, calls=%fused_computation.11.clone.1 | loop fusion | flops 16777216 | bytes 33949712 | tf_op jit(solution)/shard_map/while/body/eval_jaxpr/jit(_where)/select_n | solution.py:82
  127.1 28.6 %fusion.91 = f32[16,32,1,64]{3,2,1,0:T(1,128)S(1)} fusion(f32[16,32,64,128]{3,2,1,0:T(8,128)} %add_select_fusion.4, f32[16,32,128,1]{2,3,1,0:T(1,128)S(1)} %bitcast.175), kind=kOutput, calls=%fused_computation.138.clone.1 | convolution fusion | flops 50331648 | bytes 17170432 | tf_op jit(solution)/shard_map/while/body/eval_jaxpr/shpn,shn->shp/dot_general | solution.py:83
  156.1 8.8 %psum.18 = f32[16]{0:T(128)S(1)} all-reduce(f32[16]{0:T(128)S(1)} %get-tuple-element.705), channel_id=1, replica_groups=mesh['parts'=2,'rep'=4,'tp'=4] {'tp'}, use_global_device_ids=true, to_apply=%region_4.4 | all-reduce | flops 16 | bytes 128 | tf_op jit(solution)/shard_map/while/body/eval_jaxpr/psum | solution.py:90
  165.0 8.8 %convolution_bitcast_fusion.9 = f32[4096,16]{0,1:T(8,128)} fusion(bf16[2048,4096]{1,0:T(8,128)(2,1)} %get-tuple-element.801, f32[16,2048]{1,0:T(8,128)S(1)} %reshape.530, f32[2048]{0:T(1024)S(1)} %get-tuple-element.800, f32[16]{0:T(128)S(1)} %add_rsqrt_fusion.4), kind=kOutput, calls=%fused_computation.12.clone.1 | convolution fusion | flops 268533760 | bytes 17178688 | tf_op jit(solution)/shard_map/while/body/eval_jaxpr/dot_general | solution.py:50
  173.9 18.8 %reduce-scatter.3.cloned.1.call-done = f32[1024,16]{0,1:T(8,128)} async-done(((f32[4096,16]{0,1:T(8,128)}), f32[1024,16]{0,1:T(8,128)}) %reduce-scatter.3.cloned.1.call-update) | async-done | bytes 65552 | tf_op jit(solution)/shard_map/while/body/eval_jaxpr/reduce_scatter | solution.py:49
  192.7 0.9 fusion.92
  196.5 13.0 %add_select_fusion.4 = f32[16,32,64,128]{3,2,1,0:T(8,128)} fusion(f32[16,32,64,128]{3,2,1,0:T(8,128)} %get-tuple-element.761, f32[16,32,128]{2,1,0:T(8,128)S(1)} %convolution_bitcast_fusion.8, f32[16,32,64]{2,1,0:T(8,128)S(1)} %broadcast_multiply_fusion.4, f32[16,32]{1,0:T(8,128)S(1)} %get-tuple-element.700, pred[16]{0:T(512)(128)(4,1)S(1)} %get-tuple-element.701), kind=kLoop, calls=%fused_computation.11.clone.1 | loop fusion | flops 16777216 | bytes 33949712 | tf_op jit(solution)/shard_map/while/body/eval_jaxpr/jit(_where)/select_n | solution.py:82
  209.6 28.6 %fusion.91 = f32[16,32,1,64]{3,2,1,0:T(1,128)S(1)} fusion(f32[16,32,64,128]{3,2,1,0:T(8,128)} %add_select_fusion.4, f32[16,32,128,1]{2,3,1,0:T(1,128)S(1)} %bitcast.175), kind=kOutput, calls=%fused_computation.138.clone.1 | convolution fusion | flops 50331648 | bytes 17170432 | tf_op jit(solution)/shard_map/while/body/eval_jaxpr/shpn,shn->shp/dot_general | solution.py:83
  238.6 8.9 %psum.18 = f32[16]{0:T(128)S(1)} all-reduce(f32[16]{0:T(128)S(1)} %get-tuple-element.705), channel_id=1, replica_groups=mesh['parts'=2,'rep'=4,'tp'=4] {'tp'}, use_global_device_ids=true, to_apply=%region_4.4 | all-reduce | flops 16 | bytes 128 | tf_op jit(solution)/shard_map/while/body/eval_jaxpr/psum | solution.py:90
  247.5 8.8 %convolution_bitcast_fusion.9 = f32[4096,16]{0,1:T(8,128)} fusion(bf16[2048,4096]{1,0:T(8,128)(2,1)} %get-tuple-element.801, f32[16,2048]{1,0:T(8,128)S(1)} %reshape.530, f32[2048]{0:T(1024)S(1)} %get-tuple-element.800, f32[16]{0:T(128)S(1)} %add_rsqrt_fusion.4), kind=kOutput, calls=%fused_computation.12.clone.1 | convolution fusion | flops 268533760 | bytes 17178688 | tf_op jit(solution)/shard_map/while/body/eval_jaxpr/dot_general | solution.py:50
  256.4 18.9 %reduce-scatter.3.cloned.1.call-done = f32[1024,16]{0,1:T(8,128)} async-done(((f32[4096,16]{0,1:T(8,128)}), f32[1024,16]{0,1:T(8,128)}) %reduce-scatter.3.cloned.1.call-update) | async-done | bytes 65552 | tf_op jit(solution)/shard_map/while/body/eval_jaxpr/reduce_scatter | solution.py:49
  275.3 0.9 fusion.92
  277.9 3.3 all-to-all-start.1
  282.8 2.7 all-to-all-done.1
  285.4 3.5 all-to-all-start.2
  288.9 8.7 %gather_fusion = bf16[8,32,64,128]{3,2,1,0:T(8,128)(2,1)} fusion(f32[16,32,64,128]{3,2,1,0:T(8,128)} %get-tuple-element.223, s32[1024]{0:T(1024)S(1)} %pad_clamp_fusion), kind=kCustom, calls=%fused_computation | custom fusion | bytes 8388640 | tf_op jit(solution)/shard_map/gather | solution.py:113
  297.6 4.9 all-to-all-start
  306.1 44.6 %all-to-all-done = bf16[4,2,32,64,128]{4,3,2,1,0:T(8,128)(2,1)} async-done(((bf16[4,2,32,64,128]{4,3,2,1,0:T(8,128)(2,1)}), bf16[4,2,32,64,128]{4,3,2,1,0:T(8,128)(2,1)}, u32[]{:S(2)}, u32[]{:S(2)}) %all-to-all-start) | async-done | bytes 4194336 | tf_op jit(solution)/shard_map/all_to_all | solution.py:117
  350.7 6.5 %bitcast_convert_fusion = f32[8,32,64,128]{3,2,1,0:T(8,128)} fusion(bf16[4,2,32,64,128]{4,3,2,1,0:T(8,128)(2,1)} %all-to-all-done), kind=kLoop, calls=%fused_computation.111 | loop fusion | flops 2097152 | bytes 12582912 | tf_op jit(solution)/shard_map/reshape | solution.py:137
  357.2 13.7 %scatter_fusion = f32[16,32,64,128]{3,2,1,0:T(8,128)} fusion(f32[16,32,64,128]{3,2,1,0:T(8,128)} %get-tuple-element.223, s32[8]{0:T(128)S(1)} %fusion.46, f32[8,32,64,128]{3,2,1,0:T(8,128)} %bitcast_convert_fusion), kind=kCustom, calls=%fused_computation.4 | custom fusion | bytes 25165856 | tf_op jit(solution)/shard_map/scatter | solution.py:136
  370.9 251.3 %while.36 = (s32[]{:T(128)}, f32[16,32,64,128]{3,2,1,0:T(8,128)}, bf16[16,3,2048]{2,1,0:T(4,128)(2,1)S(1)}, bf16[16,3,2048]{2,1,0:T(4,128)(2,1)S(1)}, bf16[3,16,...) while((s32[]{:T(128)}, f32[16,32,64,128]{3,2,1,0:T(8,128)}, ...), condition=%wide.region_18.19_spmd.clone, body=%wide.region_12.18_spmd.clone.sunk | while | flops 351606848 | bytes 75476680 | solution.py:151
  371.5 1.1 multiply_reduce_fusion.12
  375.3 13.0 %add_select_fusion.5 = f32[16,32,64,128]{3,2,1,0:T(8,128)} fusion(f32[16,32,64,128]{3,2,1,0:T(8,128)} %get-tuple-element.827, f32[16,32,128]{2,1,0:T(8,128)S(1)} %convolution_bitcast_fusion.10, f32[16,32,64]{2,1,0:T(8,128)S(1)} %broadcast_multiply_fusion.5, f32[16,32]{1,0:T(8,128)S(1)} %get-tuple-element.731, pred[16]{0:T(512)(128)(4,1)S(1)} %get-tuple-element.732), kind=kLoop, calls=%fused_computation.62.clone.1 | loop fusion | flops 16777216 | bytes 33949712 | tf_op jit(solution)/shard_map/while/body/eval_jaxpr/jit(_where)/select_n | solution.py:82
  388.4 28.6 %fusion.101 = f32[16,32,1,64]{3,2,1,0:T(1,128)S(1)} fusion(f32[16,32,64,128]{3,2,1,0:T(8,128)} %add_select_fusion.5, f32[16,32,128,1]{2,3,1,0:T(1,128)S(1)} %bitcast.176), kind=kOutput, calls=%fused_computation.139.clone.1 | convolution fusion | flops 50331648 | bytes 17170432 | tf_op jit(solution)/shard_map/while/body/eval_jaxpr/shpn,shn->shp/dot_general | solution.py:83
  417.4 8.8 %psum.19 = f32[16]{0:T(128)S(1)} all-reduce(f32[16]{0:T(128)S(1)} %get-tuple-element.736), channel_id=1, replica_groups=mesh['parts'=2,'rep'=4,'tp'=4] {'tp'}, use_global_device_ids=true, to_apply=%region_16.16 | all-reduce | flops 16 | bytes 128 | tf_op jit(solution)/shard_map/while/body/eval_jaxpr/psum | solution.py:90
  426.2 8.8 %convolution_bitcast_fusion.11 = f32[4096,16]{0,1:T(8,128)} fusion(bf16[2048,4096]{1,0:T(8,128)(2,1)} %get-tuple-element.867, f32[16,2048]{1,0:T(8,128)S(1)} %reshape.532, f32[2048]{0:T(1024)S(1)} %get-tuple-element.866, f32[16]{0:T(128)S(1)} %add_rsqrt_fusion.5), kind=kOutput, calls=%fused_computation.63.clone.1 | convolution fusion | flops 268533760 | bytes 17178688 | tf_op jit(solution)/shard_map/while/body/eval_jaxpr/dot_general | solution.py:50
  435.8 17.5 %reduce-scatter.5.cloned.1.call-done = f32[1024,16]{0,1:T(8,128)} async-done(((f32[4096,16]{0,1:T(8,128)}), f32[1024,16]{0,1:T(8,128)}) %reduce-scatter.5.cloned.1.call-update) | async-done | bytes 65552 | tf_op jit(solution)/shard_map/while/body/eval_jaxpr/reduce_scatter | solution.py:49
  454.7 1.1 multiply_reduce_fusion.12
  458.6 13.0 %add_select_fusion.5 = f32[16,32,64,128]{3,2,1,0:T(8,128)} fusion(f32[16,32,64,128]{3,2,1,0:T(8,128)} %get-tuple-element.827, f32[16,32,128]{2,1,0:T(8,128)S(1)} %convolution_bitcast_fusion.10, f32[16,32,64]{2,1,0:T(8,128)S(1)} %broadcast_multiply_fusion.5, f32[16,32]{1,0:T(8,128)S(1)} %get-tuple-element.731, pred[16]{0:T(512)(128)(4,1)S(1)} %get-tuple-element.732), kind=kLoop, calls=%fused_computation.62.clone.1 | loop fusion | flops 16777216 | bytes 33949712 | tf_op jit(solution)/shard_map/while/body/eval_jaxpr/jit(_where)/select_n | solution.py:82
  471.6 28.6 %fusion.101 = f32[16,32,1,64]{3,2,1,0:T(1,128)S(1)} fusion(f32[16,32,64,128]{3,2,1,0:T(8,128)} %add_select_fusion.5, f32[16,32,128,1]{2,3,1,0:T(1,128)S(1)} %bitcast.176), kind=kOutput, calls=%fused_computation.139.clone.1 | convolution fusion | flops 50331648 | bytes 17170432 | tf_op jit(solution)/shard_map/while/body/eval_jaxpr/shpn,shn->shp/dot_general | solution.py:83
  500.7 8.8 %psum.19 = f32[16]{0:T(128)S(1)} all-reduce(f32[16]{0:T(128)S(1)} %get-tuple-element.736), channel_id=1, replica_groups=mesh['parts'=2,'rep'=4,'tp'=4] {'tp'}, use_global_device_ids=true, to_apply=%region_16.16 | all-reduce | flops 16 | bytes 128 | tf_op jit(solution)/shard_map/while/body/eval_jaxpr/psum | solution.py:90
  509.5 8.8 %convolution_bitcast_fusion.11 = f32[4096,16]{0,1:T(8,128)} fusion(bf16[2048,4096]{1,0:T(8,128)(2,1)} %get-tuple-element.867, f32[16,2048]{1,0:T(8,128)S(1)} %reshape.532, f32[2048]{0:T(1024)S(1)} %get-tuple-element.866, f32[16]{0:T(128)S(1)} %add_rsqrt_fusion.5), kind=kOutput, calls=%fused_computation.63.clone.1 | convolution fusion | flops 268533760 | bytes 17178688 | tf_op jit(solution)/shard_map/while/body/eval_jaxpr/dot_general | solution.py:50
  519.1 18.1 %reduce-scatter.5.cloned.1.call-done = f32[1024,16]{0,1:T(8,128)} async-done(((f32[4096,16]{0,1:T(8,128)}), f32[1024,16]{0,1:T(8,128)}) %reduce-scatter.5.cloned.1.call-update) | async-done | bytes 65552 | tf_op jit(solution)/shard_map/while/body/eval_jaxpr/reduce_scatter | solution.py:49
  537.2 0.9 fusion.102
  538.6 1.1 multiply_reduce_fusion.12
  542.4 13.0 %add_select_fusion.5 = f32[16,32,64,128]{3,2,1,0:T(8,128)} fusion(f32[16,32,64,128]{3,2,1,0:T(8,128)} %get-tuple-element.827, f32[16,32,128]{2,1,0:T(8,128)S(1)} %convolution_bitcast_fusion.10, f32[16,32,64]{2,1,0:T(8,128)S(1)} %broadcast_multiply_fusion.5, f32[16,32]{1,0:T(8,128)S(1)} %get-tuple-element.731, pred[16]{0:T(512)(128)(4,1)S(1)} %get-tuple-element.732), kind=kLoop, calls=%fused_computation.62.clone.1 | loop fusion | flops 16777216 | bytes 33949712 | tf_op jit(solution)/shard_map/while/body/eval_jaxpr/jit(_where)/select_n | solution.py:82
  555.5 28.6 %fusion.101 = f32[16,32,1,64]{3,2,1,0:T(1,128)S(1)} fusion(f32[16,32,64,128]{3,2,1,0:T(8,128)} %add_select_fusion.5, f32[16,32,128,1]{2,3,1,0:T(1,128)S(1)} %bitcast.176), kind=kOutput, calls=%fused_computation.139.clone.1 | convolution fusion | flops 50331648 | bytes 17170432 | tf_op jit(solution)/shard_map/while/body/eval_jaxpr/shpn,shn->shp/dot_general | solution.py:83
  584.5 8.9 %psum.19 = f32[16]{0:T(128)S(1)} all-reduce(f32[16]{0:T(128)S(1)} %get-tuple-element.736), channel_id=1, replica_groups=mesh['parts'=2,'rep'=4,'tp'=4] {'tp'}, use_global_device_ids=true, to_apply=%region_16.16 | all-reduce | flops 16 | bytes 128 | tf_op jit(solution)/shard_map/while/body/eval_jaxpr/psum | solution.py:90
  593.5 8.8 %convolution_bitcast_fusion.11 = f32[4096,16]{0,1:T(8,128)} fusion(bf16[2048,4096]{1,0:T(8,128)(2,1)} %get-tuple-element.867, f32[16,2048]{1,0:T(8,128)S(1)} %reshape.532, f32[2048]{0:T(1024)S(1)} %get-tuple-element.866, f32[16]{0:T(128)S(1)} %add_rsqrt_fusion.5), kind=kOutput, calls=%fused_computation.63.clone.1 | convolution fusion | flops 268533760 | bytes 17178688 | tf_op jit(solution)/shard_map/while/body/eval_jaxpr/dot_general | solution.py:50
  603.1 18.2 %reduce-scatter.5.cloned.1.call-done = f32[1024,16]{0,1:T(8,128)} async-done(((f32[4096,16]{0,1:T(8,128)}), f32[1024,16]{0,1:T(8,128)}) %reduce-scatter.5.cloned.1.call-update) | async-done | bytes 65552 | tf_op jit(solution)/shard_map/while/body/eval_jaxpr/reduce_scatter | solution.py:49
  (227 shorter events, 35.8 us)
Async XLA Ops:
  7.2 12.0 %copy-start.14 = (s32[1,4,4,2,2]{2,4,3,1,0:T(2,128)S(1)}, s32[1,4,4,2,2]{2,4,3,1,0:T(2,128)}, u32[]{:S(2)}) copy-start(s32[1,4,4,2,2]{2,4,3,1,0:T(2,128)} %param.39) | copy-start | bytes 772
  7.2 17.9 %copy-start.13 = (bf16[6,16,32]{2,1,0:T(8,128)(2,1)S(1)}, bf16[6,16,32]{2,1,0:T(8,128)(2,1)}, u32[]{:S(2)}) copy-start(bf16[6,16,32]{2,1,0:T(8,128)(2,1)} %param.25) | copy-start | bytes 18436
  7.2 17.9 %copy-start.7 = (bf16[6,16,2048]{2,1,0:T(8,128)(2,1)S(1)}, bf16[6,16,2048]{2,1,0:T(8,128)(2,1)}, u32[]{:S(2)}) copy-start(bf16[6,16,2048]{2,1,0:T(8,128)(2,1)} %param.23) | copy-start | bytes 1179652
  7.2 18.0 %copy-start.8 = (bf16[6,16,2048]{2,1,0:T(8,128)(2,1)S(1)}, bf16[6,16,2048]{2,1,0:T(8,128)(2,1)}, u32[]{:S(2)}) copy-start(bf16[6,16,2048]{2,1,0:T(8,128)(2,1)} %param.22) | copy-start | bytes 1179652
  7.2 18.0 %copy-start.9 = (bf16[6,16,2048]{2,1,0:T(8,128)(2,1)S(1)}, bf16[6,16,2048]{2,1,0:T(8,128)(2,1)}, u32[]{:S(2)}) copy-start(bf16[6,16,2048]{2,1,0:T(8,128)(2,1)} %param.24) | copy-start | bytes 1179652
  7.2 18.0 %copy-start = (bf16[16,3,2048]{2,0,1:T(8,128)(2,1)S(1)}, bf16[16,3,2048]{2,0,1:T(8,128)(2,1)}, u32[]{:S(2)}) copy-start(bf16[16,3,2048]{2,0,1:T(8,128)(2,1)} %param.36) | copy-start | bytes 589828
  7.2 18.0 %copy-start.1 = (bf16[16,3,2048]{2,0,1:T(8,128)(2,1)S(1)}, bf16[16,3,2048]{2,0,1:T(8,128)(2,1)}, u32[]{:S(2)}) copy-start(bf16[16,3,2048]{2,0,1:T(8,128)(2,1)} %param.37) | copy-start | bytes 589828
  7.2 18.0 %copy-start.2 = (f32[2048]{0:T(1024)S(1)}, f32[2048]{0:T(1024)}, u32[]{:S(2)}) copy-start(f32[2048]{0:T(1024)} %param.33) | copy-start | bytes 24580
  7.3 18.0 %copy-start.3 = (f32[4,2048]{1,0:T(4,128)S(1)}, f32[4,2048]{1,0:T(4,128)}, u32[]{:S(2)}) copy-start(f32[4,2048]{1,0:T(4,128)} %param.26) | copy-start | bytes 98308
  7.3 18.0 %copy-start.4 = (f32[4,2048]{1,0:T(4,128)S(1)}, f32[4,2048]{1,0:T(4,128)}, u32[]{:S(2)}) copy-start(f32[4,2048]{1,0:T(4,128)} %param.28) | copy-start | bytes 98308
  7.3 18.0 %copy-start.5 = (f32[2048]{0:T(1024)S(1)}, f32[2048]{0:T(1024)}, u32[]{:S(2)}) copy-start(f32[2048]{0:T(1024)} %param.27) | copy-start | bytes 24580
  7.3 18.0 %copy-start.6 = (f32[2048]{0:T(1024)S(1)}, f32[2048]{0:T(1024)}, u32[]{:S(2)}) copy-start(f32[2048]{0:T(1024)} %param.29) | copy-start | bytes 24580
  7.3 18.0 %copy-start.10 = (f32[32]{0:T(128)S(1)}, f32[32]{0:T(128)}, u32[]{:S(2)}) copy-start(f32[32]{0:T(128)} %param.32) | copy-start | bytes 388
  7.3 18.0 %copy-start.11 = (f32[32]{0:T(128)S(1)}, f32[32]{0:T(128)}, u32[]{:S(2)}) copy-start(f32[32]{0:T(128)} %param.30) | copy-start | bytes 388
  7.3 18.0 %copy-start.12 = (f32[32]{0:T(128)S(1)}, f32[32]{0:T(128)}, u32[]{:S(2)}) copy-start(f32[32]{0:T(128)} %param.31) | copy-start | bytes 388
  20.9 257.0 %all-to-all-start.3 = ((bf16[4,1,2]{2,1,0:T(2,128)(2,1)}), bf16[4,1,2]{2,1,0:T(2,128)(2,1)S(1)}, u32[]{:S(2)}, u32[]{:S(2)}) async-start(bf16[4,1,2]{2,1,0:T(2,128)(2,1)} %copy.82), calls=%async_computation.5 | async-start | bytes 4096 | tf_op jit(solution)/shard_map/all_to_all | solution.py:126
  25.4 84.8 %reduce-scatter.3.cloned.1.call-start = ((), (), s32[]{:S(2)}) async-start(), calls=%async_computation.6 | async-start | bytes 327680 | tf_op jit(solution)/shard_map/while/body/eval_jaxpr/reduce_scatter | solution.py:49
  111.1 81.6 %reduce-scatter.3.cloned.1.call-start = ((), (), s32[]{:S(2)}) async-start(), calls=%async_computation.6 | async-start | bytes 327680 | tf_op jit(solution)/shard_map/while/body/eval_jaxpr/reduce_scatter | solution.py:49
  193.6 81.8 %reduce-scatter.3.cloned.1.call-start = ((), (), s32[]{:S(2)}) async-start(), calls=%async_computation.6 | async-start | bytes 327680 | tf_op jit(solution)/shard_map/while/body/eval_jaxpr/reduce_scatter | solution.py:49
  277.9 7.6 %all-to-all-start.1 = ((bf16[4,2,3,2048]{3,1,2,0:T(2,128)(2,1)}), bf16[4,2,3,2048]{3,1,2,0:T(2,128)(2,1)S(1)}, u32[]{:S(2)}, u32[]{:S(2)}) async-start(bf16[4,2,3,2048]{3,1,2,0:T(2,128)(2,1)} %copy.71), calls=%async_computation.3 | async-start | bytes 196608 | tf_op jit(solution)/shard_map/all_to_all | solution.py:120
  285.4 12.1 %all-to-all-start.2 = ((bf16[4,2,3,2048]{3,1,2,0:T(2,128)(2,1)}), bf16[4,2,3,2048]{3,1,2,0:T(2,128)(2,1)S(1)}, u32[]{:S(2)}, u32[]{:S(2)}) async-start(bf16[4,2,3,2048]{3,1,2,0:T(2,128)(2,1)} %copy.76), calls=%async_computation.4 | async-start | bytes 196608 | tf_op jit(solution)/shard_map/all_to_all | solution.py:123
  297.6 53.2 %all-to-all-start = ((bf16[4,2,32,64,128]{4,3,2,1,0:T(8,128)(2,1)}), bf16[4,2,32,64,128]{4,3,2,1,0:T(8,128)(2,1)}, u32[]{:S(2)}, u32[]{:S(2)}) async-start(bf16[4,2,32,64,128]{4,3,2,1,0:T(8,128)(2,1)} %bitcast.179), calls=%async_computation.2 | async-start | bytes 8388608 | tf_op jit(solution)/shard_map/all_to_all | solution.py:117
  370.9 82.4 %reduce-scatter.5.cloned.1.call-start = ((), (), s32[]{:S(2)}) async-start(), calls=%async_computation.7 | async-start | bytes 327680 | tf_op jit(solution)/shard_map/while/body/eval_jaxpr/reduce_scatter | solution.py:49
  454.2 83.0 %reduce-scatter.5.cloned.1.call-start = ((), (), s32[]{:S(2)}) async-start(), calls=%async_computation.7 | async-start | bytes 327680 | tf_op jit(solution)/shard_map/while/body/eval_jaxpr/reduce_scatter | solution.py:49
  538.1 83.2 %reduce-scatter.5.cloned.1.call-start = ((), (), s32[]{:S(2)}) async-start(), calls=%async_computation.7 | async-start | bytes 327680 | tf_op jit(solution)/shard_map/while/body/eval_jaxpr/reduce_scatter | solution.py:49
Sparse Core Ops, SparseCore 0:
  91.8 18.3 reduce-scatter.2
  173.9 18.7 reduce-scatter.2
  256.5 18.8 reduce-scatter.2
  435.2 18.1 reduce-scatter.4
  518.4 18.7 reduce-scatter.4
  602.4 18.8 reduce-scatter.4
where the time goes:
time: 631 us; the launch traced here: 630 us
  matrix products  229 us (36%)
  waiting for transfers between devices  157 us (25%)
  other arithmetic  105 us (17%)
  blocking collectives  56.6 us (9%)
  local copies, waits for them, and re-layouts  51.3 us (8%)
  starting transfers between devices  16 us (3%)
  between operations  13.8 us (2%)
    dot_general x6, matrix products, advance(): jnp.einsum('shpn,shn->shp', states, c_heads, precision=lax.Precision.HIGH...  172 us
    reduce_scatter x6, waiting for transfers between devices, project(): lax.psum_scatter(lax.dot_general(out_weight, hidden, (((0,), (1,)), ((),...  110 us
    select_n x6, other arithmetic, advance(): states = jnp.where(is_live[:, None, None, None], updated, states)  78.3 us
    psum x6, blocking collectives, advance(): sum_total = lax.psum(local_squares, 'tp')  56.6 us
    dot_general x6, matrix products, project(): lax.dot_general(out_weight, hidden, (((0,), (1,)), ((), ())), preferred_e...  52.8 us
    all_to_all x1, waiting for transfers between devices, body(): lax.all_to_all(sent_states.astype(jnp.bfloat16), 'rep', split_axis=0, con...  44.6 us
    scatter x1, local copies, waits for them, and re-layouts, body(): migrate_states.at[target]  13.7 us
    unnamed x32, local copies, waits for them, and re-layouts  12.6 us
  transfers between devices with their start and end apart: 10, of which 8 were waited for; matrix products, arithmetic and copies ran while one was open for 29% of the time, Pallas kernels for 0%

commit v1 on v0

v1 whole, which is shorter than its diff:
```python
import functools

import jax
import jax.numpy as jnp
from jax import lax
from jax.experimental import pallas as pl
from jax.experimental.pallas import tpu as pltpu
from jax.sharding import PartitionSpec as P

HEADS = 128
HEAD_DIM = 64
STATE = 128
GROUPS = 8
PERIOD = 3
CAP = 2
INNER = 8192
EPS = 1e-05
BF16 = jnp.bfloat16
F32 = jnp.float32
MESH = pl.DeviceIdType.MESH


def silu(v):
    return v / (1.0 + jnp.exp(-v))


def softplus(v):
    return jnp.maximum(v, 0.0) + jnp.log1p(jnp.exp(-jnp.abs(v)))


def dot(a, b):
    return lax.dot_general(a, b, (((1,), (0,)), ((), ())), preferred_element_type=F32)


def pack_matrix(slots, moved, peers, pick):
    rows, cols = 16 * peers, moved * slots
    row = lax.broadcasted_iota(jnp.int32, (rows, cols), 0)
    col = lax.broadcasted_iota(jnp.int32, (rows, cols), 1)
    halves = []
    for half in range(2):
        hit = jnp.zeros((rows, cols), F32)
        for o in range(peers):
            for c in range(CAP):
                slot = pick(o, c)
                first = o * 16 + half * CAP * moved + c * moved
                for k in range(moved):
                    match = jnp.where(row == first + k, col, -1) == k * slots + slot
                    valid = jnp.where(slot >= 0, 1.0, 0.0)
                    hit = hit + jnp.where(match, valid, 0.0)
        halves.append(hit.astype(BF16))
    return halves


def unpack_matrix(slots, moved, peers, pick):
    rows, cols = moved * slots, 16 * peers
    row = lax.broadcasted_iota(jnp.int32, (rows, cols), 0)
    col = lax.broadcasted_iota(jnp.int32, (rows, cols), 1)
    halves = []
    for half in range(2):
        hit = jnp.zeros((rows, cols), F32)
        for o in range(peers):
            for c in range(CAP):
                slot = pick(o, c)
                first = o * 16 + half * CAP * moved + c * moved
                for k in range(moved):
                    match = jnp.where(col == first + k, row, -1) == k * slots + slot
                    valid = jnp.where(slot >= 0, 1.0, 0.0)
                    hit = hit + jnp.where(match, valid, 0.0)
        halves.append(hit.astype(BF16))
    return halves


def named(slots, peers, pick):
    row = lax.broadcasted_iota(jnp.int32, (slots, 1), 0)
    hit = jnp.zeros((slots, 1), F32)
    for o in range(peers):
        for c in range(CAP):
            hit = jnp.maximum(hit, jnp.where(row == pick(o, c), 1.0, 0.0))
    return hit


def kernel(
    dims,
    gate_ref,
    conv_ref,
    bc_ref,
    delta_ref,
    conv_w_ref,
    conv_b_ref,
    bc_w_ref,
    bc_b_ref,
    delta_b_ref,
    decay_ref,
    skip_ref,
    gain_ref,
    w_hbm,
    state_hbm,
    conv_state_ref,
    bc_state_ref,
    finish_ref,
    plan_ref,
    out_ref,
    st,
    wv,
    msg,
    got,
    xs,
    bs,
    cs,
    y0,
    gates,
    hidden,
    sq_mine,
    sq_got,
    part,
    part_got,
    rows_out,
    back,
    back_got,
    st_sem,
    w_sem,
    msg_send,
    msg_recv,
    sq_send,
    sq_recv,
    part_send,
    part_recv,
    back_send,
    back_recv,
):
    T, S, IL, HL, NG, R, TP, DL = dims
    GH = HL // NG
    GC = NG * 2 * STATE
    moved = T - PERIOD
    M = moved * S
    me = lax.axis_index("rep")
    tp = lax.axis_index("tp")

    def state_copy(s):
        return pltpu.make_async_copy(state_hbm.at[s], st.at[s], st_sem.at[s])

    def w_copy(o):
        column = pl.multiple_of(lax.rem(tp + o, TP) * DL, DL)
        return pltpu.make_async_copy(w_hbm.at[:, pl.ds(column, DL)], wv.at[o], w_sem.at[o])

    for s in range(S):
        state_copy(s).start()
    for o in list(range(1, TP)) + [0]:
        w_copy(o).start()

    barrier = pltpu.get_barrier_semaphore()
    for o in range(1, R):
        pl.semaphore_signal(
            barrier, inc=1, device_id={"rep": lax.rem(me + o, R)}, device_id_type=MESH
        )
    for o in range(1, TP):
        pl.semaphore_signal(
            barrier, inc=1, device_id={"tp": lax.rem(tp + o, TP)}, device_id_type=MESH
        )

    def entry(source, target, c, which):
        return plan_ref[((source * R + target) * CAP + c) * 2 + which]

    def ahead(o):
        return lax.rem(me + (o + 1), R)

    def behind(o):
        return lax.rem(me + (R - 1 - o), R)

    serve_send = lambda o, c: entry(ahead(o), me, c, 1)
    serve_take = lambda o, c: entry(me, behind(o), c, 0)
    give_send = lambda o, c: entry(me, ahead(o), c, 0)
    give_take = lambda o, c: entry(behind(o), me, c, 1)

    group_column = pl.multiple_of((tp * HL * GROUPS // HEADS) * 2 * STATE, 2 * STATE)
    group_cols = pl.ds(group_column, GC)

    pack_a, pack_b = pack_matrix(S, moved, R - 1, serve_send)
    gate_rows = gate_ref[PERIOD:].reshape(M, IL)
    conv_rows = conv_ref[PERIOD:].reshape(M, IL)
    bc_rows = bc_ref[PERIOD:, :, group_cols].reshape(M, GC)
    delta_rows = delta_ref[PERIOD:].reshape(M, HL)
    packed = dot(pack_a, gate_rows) + dot(pack_b, conv_rows)
    msg[:, :, 0:IL] = packed.astype(BF16).reshape(R - 1, 16, IL)
    msg[:, :, IL : IL + GC] = dot(pack_a, bc_rows).astype(BF16).reshape(R - 1, 16, GC)
    pad_rows = jnp.concatenate([delta_rows.astype(F32), jnp.zeros((M, 128 - HL), F32)], axis=1)
    msg[:, :, IL + GC :] = dot(pack_a, pad_rows.astype(BF16)).astype(BF16).reshape(R - 1, 16, 128)

    pl.semaphore_wait(barrier, R - 1 + TP - 1)

    def msg_copy(o):
        return pltpu.make_async_remote_copy(
            src_ref=msg.at[o],
            dst_ref=got.at[o],
            send_sem=msg_send.at[o],
            recv_sem=msg_recv.at[o],
            device_id={"rep": ahead(o)},
            device_id_type=MESH,
        )

    for o in range(R - 1):
        msg_copy(o).start()

    take_a, take_b = unpack_matrix(S, moved, R - 1, serve_take)
    is_source = named(S, R - 1, serve_take)
    is_target = named(S, R - 1, give_take)
    own = 1.0 - is_source
    own_rows = jnp.concatenate([own] * moved, axis=0)

    conv_old = conv_state_ref[...].astype(F32)
    bc_old = bc_state_ref[:, :, group_cols].astype(F32)

    for o in range(R - 1):
        msg_copy(o).wait()
    arrived = got[...].reshape((R - 1) * 16, IL + GC + 128)
    new_gate = dot(take_a, arrived[:, 0:IL]) + own_rows * gate_rows.astype(F32)
    new_conv = dot(take_b, arrived[:, 0:IL]) + own_rows * conv_rows.astype(F32)
    tail = dot(take_a, arrived[:, IL:])
    new_bc = tail[:, 0:GC] + own_rows * bc_rows.astype(F32)
    new_delta = tail[:, GC : GC + HL] + own_rows * delta_rows.astype(F32)

    gates[0:M] = gate_ref[0:PERIOD].reshape(M, IL).astype(F32)
    gates[M:] = new_gate

    seq = [conv_old[:, k, :] for k in range(3)]
    seq += [conv_ref[t].astype(F32) for t in range(PERIOD)]
    seq += [new_conv[k * S : (k + 1) * S] for k in range(moved)]
    for t in range(T):
        mixed = conv_b_ref[...]
        for k in range(4):
            mixed = mixed + conv_w_ref[k : k + 1, :] * seq[t + k]
        xs[t * S : (t + 1) * S] = silu(mixed)

    seq = [bc_old[:, k, :] for k in range(3)]
    seq += [bc_ref[t, :, group_cols].astype(F32) for t in range(PERIOD)]
    seq += [new_bc[k * S : (k + 1) * S] for k in range(moved)]
    for t in range(T):
        mixed = bc_b_ref[:, group_cols]
        for k in range(4):
            mixed = mixed + bc_w_ref[k : k + 1, group_cols] * seq[t + k]
        act = silu(mixed)
        for g in range(NG):
            low = g * 2 * STATE
            bs[t, :, g * STATE : (g + 1) * STATE] = act[:, low : low + STATE]
            cs[t, :, g * STATE : (g + 1) * STATE] = act[:, low + STATE : low + 2 * STATE]
    for t in range(T, 8):
        cs[t] = jnp.zeros((S, NG * STATE), F32)

    def one_slot(s, _):
        state_copy(s).wait()
        rows8 = cs[:, s, :]
        for g in range(NG):
            cg = rows8[:, g * STATE : (g + 1) * STATE]
            high = cg.astype(BF16).astype(F32)
            lhs = jnp.concatenate([high, cg - high], axis=0).astype(BF16)
            held = st[s, g * GH : (g + 1) * GH].reshape(GH * HEAD_DIM, STATE).astype(BF16)
            both = lax.dot_general(
                lhs, held, (((1,), (1,)), ((), ())), preferred_element_type=F32
            )
            y0[:, s, g * GH * HEAD_DIM : (g + 1) * GH * HEAD_DIM] = both[0:8] + both[8:16]
        return 0

    lax.fori_loop(0, S, one_slot, 0)

    finish = finish_ref[...]
    live = [jnp.where(finish > t, 1.0, 0.0) for t in range(T)]
    steps, keeps = [], []
    for t in range(T):
        if t < PERIOD:
            raw = delta_ref[t].astype(F32)
        else:
            raw = new_delta[(t - PERIOD) * S : (t - PERIOD + 1) * S]
        size = softplus(raw + delta_b_ref[...]) * live[t]
        steps.append(size)
        keeps.append(jnp.exp(-size * decay_ref[...]))

    head = lax.broadcasted_iota(jnp.int32, (S, HL), 1)
    spread_row = lax.broadcasted_iota(jnp.int32, (2 * HL, IL), 0)
    spread_col = lax.broadcasted_iota(jnp.int32, (2 * HL, IL), 1)
    spread_from = jnp.where(spread_row >= HL, spread_row - HL, spread_row) * HEAD_DIM
    offset = spread_col - spread_from
    spread = jnp.where((offset >= 0) & (offset < HEAD_DIM), 1.0, 0.0).astype(BF16)

    start = None
    weights = []
    lane = lax.broadcasted_iota(jnp.int32, (S, 128), 1)
    squares = jnp.zeros((S, 128), F32)
    for t in range(T):
        start = keeps[t] if t == 0 else start * keeps[t]
        weights = [w * keeps[t] for w in weights] + [steps[t]]
        blocks = [start]
        for u in range(t + 1):
            scores = jnp.zeros((S, HL), F32)
            for g in range(NG):
                span = slice(g * STATE, (g + 1) * STATE)
                score = jnp.sum(cs[t, :, span] * bs[u, :, span], axis=1, keepdims=True)
                inside = (head >= g * GH) & (head < (g + 1) * GH)
                scores = jnp.where(inside, score, scores)
            block = weights[u] * scores
            if u == t:
                block = block + skip_ref[...]
            blocks.append(block)
        table = jnp.concatenate(blocks, axis=0)
        high = table.astype(BF16).astype(F32)
        table = jnp.concatenate([high, table - high], axis=1).astype(BF16)
        width = min(IL, 512)
        square = jnp.zeros((S, 1), F32)
        for low in range(0, IL, width):
            cols = slice(low, low + width)
            wide = dot(table, spread[:, cols])
            total = wide[0:S] * y0[t, :, cols]
            for u in range(t + 1):
                total = total + wide[(u + 1) * S : (u + 2) * S] * xs[u * S : (u + 1) * S, cols]
            gated = total * silu(gates[t * S : (t + 1) * S, cols])
            square = square + jnp.sum(gated * gated, axis=1, keepdims=True)
            hidden[t * S : (t + 1) * S, cols] = (gated * gain_ref[:, cols]).astype(BF16)
        squares = jnp.where(lane == t, square, squares)

    sq_mine[...] = squares

    def sq_copy(o):
        return pltpu.make_async_remote_copy(
            src_ref=sq_mine,
            dst_ref=sq_got.at[o],
            send_sem=sq_send.at[o],
            recv_sem=sq_recv.at[o],
            device_id={"tp": lax.rem(tp + (o + 1), TP)},
            device_id_type=MESH,
        )

    for o in range(TP - 1):
        sq_copy(o).start()

    def part_copy(o):
        return pltpu.make_async_remote_copy(
            src_ref=part.at[o],
            dst_ref=part_got.at[o],
            send_sem=part_send.at[o],
            recv_sem=part_recv.at[o],
            device_id={"tp": lax.rem(tp + (o + 1), TP)},
            device_id_type=MESH,
        )

    for o in range(1, TP):
        w_copy(o).wait()
        part[o - 1] = dot(hidden[...], wv[o]).astype(BF16)
        part_copy(o - 1).start()
    w_copy(0).wait()
    total = dot(hidden[...], wv[0])

    for o in range(TP - 1):
        sq_copy(o).wait()
        squares = squares + sq_got[o]
    inv_rms = lax.rsqrt(squares / INNER + EPS)
    scale = jnp.concatenate([inv_rms[:, t : t + 1] * live[t] for t in range(T)], axis=0)

    for o in range(TP - 1):
        part_copy(o).wait()
        total = total + part_got[o].astype(F32)
    rows_out[...] = (total * scale).astype(BF16)

    half = DL // 2
    give_a, give_b = pack_matrix(S, moved, R - 1, give_send)
    later = rows_out[M:, :]
    packed = dot(give_a, later[:, 0:half]) + dot(give_b, later[:, half:])
    back[...] = packed.astype(BF16).reshape(R - 1, 16, half)

    def back_copy(o):
        return pltpu.make_async_remote_copy(
            src_ref=back.at[o],
            dst_ref=back_got.at[o],
            send_sem=back_send.at[o],
            recv_sem=back_recv.at[o],
            device_id={"rep": ahead(o)},
            device_id_type=MESH,
        )

    for o in range(R - 1):
        back_copy(o).start()
    out_ref[0:PERIOD] = rows_out[0:M, :].reshape(PERIOD, S, DL)
    put_a, put_b = unpack_matrix(S, moved, R - 1, give_take)
    keep = own * (1.0 - is_target)
    keep_rows = jnp.concatenate([keep] * moved, axis=0)
    stay = keep_rows * later.astype(F32)
    for o in range(R - 1):
        back_copy(o).wait()
    arrived = back_got[...].reshape((R - 1) * 16, half)
    left = (dot(put_a, arrived) + stay[:, 0:half]).astype(BF16)
    right = (dot(put_b, arrived) + stay[:, half:]).astype(BF16)
    out_ref[PERIOD:, :, 0:half] = left.reshape(moved, S, half)
    out_ref[PERIOD:, :, half:] = right.reshape(moved, S, half)


def body(R, TP, *arrays):
    (gate, conv, bc, delta, conv_w, conv_b, bc_w, bc_b, delta_b, decay, skip, gain, w, state,
     conv_state, bc_state, finish, plan) = arrays
    T, S, IL = gate.shape
    HL = delta.shape[2]
    NG = max(1, HL * GROUPS // HEADS)
    D = w.shape[1]
    DL = D // TP
    GC = NG * 2 * STATE
    wide = IL + GC + 128
    dims = (T, S, IL, HL, NG, R, TP, DL)
    vmem = pl.BlockSpec(memory_space=pltpu.VMEM)
    hbm = pl.BlockSpec(memory_space=pl.ANY)
    smem = pl.BlockSpec(memory_space=pltpu.SMEM)
    dma = pltpu.SemaphoreType.DMA
    half = DL // 2
    return pl.pallas_call(
        functools.partial(kernel, dims),
        out_shape=jax.ShapeDtypeStruct((T, S, DL), BF16),
        in_specs=[vmem] * 12 + [hbm, hbm] + [vmem] * 3 + [smem],
        out_specs=vmem,
        scratch_shapes=[
            pltpu.VMEM((S, HL, HEAD_DIM, STATE), F32),
            pltpu.VMEM((TP, IL, DL), BF16),
            pltpu.VMEM((R - 1, 16, wide), BF16),
            pltpu.VMEM((R - 1, 16, wide), BF16),
            pltpu.VMEM((T * S, IL), F32),
            pltpu.VMEM((8, S, NG * STATE), F32),
            pltpu.VMEM((8, S, NG * STATE), F32),
            pltpu.VMEM((8, S, IL), F32),
            pltpu.VMEM((T * S, IL), F32),
            pltpu.VMEM((T * S, IL), BF16),
            pltpu.VMEM((S, 128), F32),
            pltpu.VMEM((TP - 1, S, 128), F32),
            pltpu.VMEM((TP - 1, T * S, DL), BF16),
            pltpu.VMEM((TP - 1, T * S, DL), BF16),
            pltpu.VMEM((T * S, DL), BF16),
            pltpu.VMEM((R - 1, 16, half), BF16),
            pltpu.VMEM((R - 1, 16, half), BF16),
            dma((S,)),
            dma((TP,)),
            dma((R - 1,)),
            dma((R - 1,)),
            dma((TP - 1,)),
            dma((TP - 1,)),
            dma((TP - 1,)),
            dma((TP - 1,)),
            dma((R - 1,)),
            dma((R - 1,)),
        ],
        compiler_params=pltpu.CompilerParams(
            collective_id=0, has_side_effects=True, vmem_limit_bytes=58 * 1024 * 1024
        ),
    )(
        gate,
        conv,
        bc,
        delta,
        conv_w,
        conv_b.reshape(1, -1),
        bc_w,
        bc_b.reshape(1, -1),
        delta_b.reshape(1, -1),
        decay.reshape(1, -1),
        skip.reshape(1, -1),
        gain.reshape(1, -1),
        w,
        state,
        conv_state,
        bc_state,
        finish.reshape(-1, 1),
        plan.reshape(-1),
    )


def solution(mesh):
    rows = ("parts", "rep")
    in_specs = (
        P(None, rows, "tp"),
        P(None, rows, "tp"),
        P(None, rows, None),
        P(None, rows, "tp"),
        P(None, "tp"),
        P("tp"),
        P(),
        P(),
        P("tp"),
        P("tp"),
        P("tp"),
        P("tp"),
        P("tp", None),
        P(rows, "tp", None, None),
        P(rows, None, "tp"),
        P(rows, None, None),
        P(rows),
        P("parts", None, None, None, None),
    )
    return jax.shard_map(
        functools.partial(body, mesh.shape["rep"], mesh.shape["tp"]),
        mesh=mesh,
        in_specs=in_specs,
        out_specs=P(None, rows, "tp"),
        check_vma=False,
    )
```

time: 631 us -> 48 us (0.08)
  the two profiles are of different devices: /device:TPU:0 before, /device:TPU:13 now
where the time goes in v1:
time: 48 us; the launch traced here: 47.8 us
  Pallas kernels  39.7 us (83%)
  local copies, waits for them, and re-layouts  8.02 us (17%)
    pallas_call x1, Pallas kernels, body(): pl.pallas_call(functools.partial(kernel, dims), out_shape=jax.ShapeDtypeS...  39.7 us
    unnamed x4, local copies, waits for them, and re-layouts  6.03 us
    reshape x1, local copies, waits for them, and re-layouts, body(): finish.reshape(-1, 1)  1.33 us

profile of v1, /device:TPU:13, one launch (start us, length us, event | category | flops | bytes accessed | tf_op | source)
XLA Modules:
  0.0 47.8 jit_solution(7994320413703848312)
XLA Ops:
  0.0 1.3 %copy.26.finish_ref = s32[16,1]{1,0:T(8,128)} copy(s32[16,1]{0,1:T(1,128)} %bitcast.10) | data formatting | bytes 128 | tf_op jit(solution)/shard_map/reshape | solution.py:464
  1.3 0.8 %copy.23 = s32[1,4,4,2,2]{4,3,2,1,0:T(2,128)S(1)} copy(s32[1,4,4,2,2]{2,4,3,1,0:T(2,128)} %param.35) | data formatting | bytes 512 | tf_op args[17]
  2.2 0.7 %reshape.31.plan_ref = s32[64]{0:T(128)} reshape(s32[1,4,4,2,2]{4,3,2,1,0:T(2,128)S(1)} %copy.23) | data formatting | bytes 512 | tf_op jit(solution)/shard_map/reshape | solution.py:465
  2.8 1.8 %copy.24.conv_state_ref = bf16[16,3,2048]{2,1,0:T(4,128)(2,1)} copy(bf16[16,3,2048]{2,0,1:T(8,128)(2,1)} %param.32) | data formatting | bytes 393216 | tf_op args[14]
  4.6 1.8 %copy.25.bc_state_ref = bf16[16,3,2048]{2,1,0:T(4,128)(2,1)} copy(bf16[16,3,2048]{2,0,1:T(8,128)(2,1)} %param.33) | data formatting | bytes 393216 | tf_op args[15]
  6.4 39.7 %shard_map.172 = bf16[6,16,1024]{2,1,0:T(8,128)(2,1)} custom-call(bf16[6,16,2048]{2,1,0:T(8,128)(2,1)} %gate_ref.1, bf16[6,16,2048]{2,1,0:T(8,128)(2,1)} %conv_ref.1, bf16[6,16,2048]{2,1,0:T(8,128)(2,1)} %bc_ref.1, bf16[6,16,32]{2,1,0:T(8,128)(2,1)} %delta_ref.1, f32[4,2048]{1,0:T(4,128)} %conv_w_ref.1, f32[1,2048]{1,0:T(1,128)} %bitcast.7, ...), custom_call_target="tpu_custom_call" | custom-call | tf_op jit(solution)/shard_map/pallas_call | solution.py:410
  46.2 1.6 %copy.28 = bf16[6,16,1024]{2,1,0:T(8,128)(2,1)} copy(bf16[6,16,1024]{2,1,0:T(8,128)(2,1)} %shard_map.172) | data formatting | bytes 393216

commit v2 on v1

v2 whole, which is shorter than its diff:
```python
import functools

import jax
import jax.numpy as jnp
from jax import lax
from jax.experimental import pallas as pl
from jax.experimental.pallas import tpu as pltpu
from jax.sharding import PartitionSpec as P

HEADS = 128
HEAD_DIM = 64
STATE = 128
GROUPS = 8
PERIOD = 3
CAP = 2
INNER = 8192
EPS = 1e-05
BF16 = jnp.bfloat16
F32 = jnp.float32
MESH = pl.DeviceIdType.MESH


def silu(v):
    return v / (1.0 + jnp.exp(-v))


def softplus(v):
    return jnp.maximum(v, 0.0) + jnp.log1p(jnp.exp(-jnp.abs(v)))


def dot(a, b):
    return lax.dot_general(a, b, (((1,), (0,)), ((), ())), preferred_element_type=F32)


def pack_matrix(slots, moved, peers, pick):
    rows, cols = 16 * peers, moved * slots
    row = lax.broadcasted_iota(jnp.int32, (rows, cols), 0)
    col = lax.broadcasted_iota(jnp.int32, (rows, cols), 1)
    halves = []
    for half in range(2):
        hit = jnp.zeros((rows, cols), F32)
        for o in range(peers):
            for c in range(CAP):
                slot = pick(o, c)
                first = o * 16 + half * CAP * moved + c * moved
                for k in range(moved):
                    match = jnp.where(row == first + k, col, -1) == k * slots + slot
                    valid = jnp.where(slot >= 0, 1.0, 0.0)
                    hit = hit + jnp.where(match, valid, 0.0)
        halves.append(hit.astype(BF16))
    return halves


def unpack_matrix(slots, moved, peers, pick):
    rows, cols = moved * slots, 16 * peers
    row = lax.broadcasted_iota(jnp.int32, (rows, cols), 0)
    col = lax.broadcasted_iota(jnp.int32, (rows, cols), 1)
    halves = []
    for half in range(2):
        hit = jnp.zeros((rows, cols), F32)
        for o in range(peers):
            for c in range(CAP):
                slot = pick(o, c)
                first = o * 16 + half * CAP * moved + c * moved
                for k in range(moved):
                    match = jnp.where(col == first + k, row, -1) == k * slots + slot
                    valid = jnp.where(slot >= 0, 1.0, 0.0)
                    hit = hit + jnp.where(match, valid, 0.0)
        halves.append(hit.astype(BF16))
    return halves


def named(slots, peers, pick):
    row = lax.broadcasted_iota(jnp.int32, (slots, 1), 0)
    hit = jnp.zeros((slots, 1), F32)
    for o in range(peers):
        for c in range(CAP):
            hit = jnp.maximum(hit, jnp.where(row == pick(o, c), 1.0, 0.0))
    return hit


def kernel(
    dims,
    gate_ref,
    conv_ref,
    bc_ref,
    delta_ref,
    conv_w_ref,
    conv_b_ref,
    bc_w_ref,
    bc_b_ref,
    delta_b_ref,
    decay_ref,
    skip_ref,
    gain_ref,
    w_hbm,
    state_hbm,
    conv_state_ref,
    bc_state_ref,
    finish_ref,
    plan_ref,
    out_ref,
    st,
    wv,
    msg,
    got,
    xs,
    bs,
    cs,
    y0,
    new_gates,
    hidden,
    sq_mine,
    sq_got,
    own_part,
    part,
    part_got,
    back,
    back_got,
    st_sem,
    w_sem,
    msg_send,
    msg_recv,
    sq_send,
    sq_recv,
    part_send,
    part_recv,
    back_send,
    back_recv,
):
    T, S, IL, HL, NG, R, TP, DL = dims
    GH = HL // NG
    GC = NG * 2 * STATE
    moved = T - PERIOD
    M = moved * S
    me = lax.axis_index("rep")
    tp = lax.axis_index("tp")

    def state_copy(s):
        return pltpu.make_async_copy(state_hbm.at[s], st.at[s], st_sem.at[s])

    def w_copy(o):
        column = pl.multiple_of(lax.rem(tp + o, TP) * DL, DL)
        return pltpu.make_async_copy(w_hbm.at[:, pl.ds(column, DL)], wv.at[o], w_sem.at[o])

    barrier = pltpu.get_barrier_semaphore()
    for o in range(1, R):
        pl.semaphore_signal(
            barrier, inc=1, device_id={"rep": lax.rem(me + o, R)}, device_id_type=MESH
        )
    for o in range(1, TP):
        pl.semaphore_signal(
            barrier, inc=1, device_id={"tp": lax.rem(tp + o, TP)}, device_id_type=MESH
        )

    for s in range(S):
        state_copy(s).start()
    for o in list(range(1, TP)) + [0]:
        w_copy(o).start()

    def entry(source, target, c, which):
        return plan_ref[source * CAP + c, which, target]

    def ahead(o):
        return lax.rem(me + (o + 1), R)

    def behind(o):
        return lax.rem(me + (R - 1 - o), R)

    serve_send = lambda o, c: entry(ahead(o), me, c, 1)
    serve_take = lambda o, c: entry(me, behind(o), c, 0)
    give_send = lambda o, c: entry(me, ahead(o), c, 0)
    give_take = lambda o, c: entry(behind(o), me, c, 1)

    group_column = pl.multiple_of((tp * HL * GROUPS // HEADS) * 2 * STATE, 2 * STATE)
    group_cols = pl.ds(group_column, GC)

    pack_a, pack_b = pack_matrix(S, moved, R - 1, serve_send)
    gate_rows = gate_ref[PERIOD:].reshape(M, IL)
    conv_rows = conv_ref[PERIOD:].reshape(M, IL)
    bc_rows = bc_ref[PERIOD:, :, group_cols].reshape(M, GC)
    delta_rows = delta_ref[PERIOD:].reshape(M, HL)
    packed = dot(pack_a, gate_rows) + dot(pack_b, conv_rows)
    msg[:, :, 0:IL] = packed.astype(BF16).reshape(R - 1, 16, IL)
    msg[:, :, IL : IL + GC] = dot(pack_a, bc_rows).astype(BF16).reshape(R - 1, 16, GC)
    pad_rows = jnp.concatenate([delta_rows.astype(F32), jnp.zeros((M, 128 - HL), F32)], axis=1)
    msg[:, :, IL + GC :] = dot(pack_a, pad_rows.astype(BF16)).astype(BF16).reshape(R - 1, 16, 128)

    pl.semaphore_wait(barrier, R - 1 + TP - 1)

    def msg_copy(o):
        return pltpu.make_async_remote_copy(
            src_ref=msg.at[o],
            dst_ref=got.at[o],
            send_sem=msg_send.at[o],
            recv_sem=msg_recv.at[o],
            device_id={"rep": ahead(o)},
            device_id_type=MESH,
        )

    for o in range(R - 1):
        msg_copy(o).start()

    def sq_copy(h, o):
        return pltpu.make_async_remote_copy(
            src_ref=sq_mine.at[h],
            dst_ref=sq_got.at[h, o],
            send_sem=sq_send.at[h, o],
            recv_sem=sq_recv.at[h, o],
            device_id={"tp": lax.rem(tp + (o + 1), TP)},
            device_id_type=MESH,
        )

    def part_copy(h, o):
        return pltpu.make_async_remote_copy(
            src_ref=part.at[h, o],
            dst_ref=part_got.at[h, o],
            send_sem=part_send.at[h, o],
            recv_sem=part_recv.at[h, o],
            device_id={"tp": lax.rem(tp + (o + 1), TP)},
            device_id_type=MESH,
        )

    slot_row = lax.broadcasted_iota(jnp.int32, (S, 1), 0)
    finish = jnp.zeros((S, 1), jnp.int32)
    for s in range(S):
        finish = jnp.where(slot_row == s, finish_ref[s], finish)
    live = [jnp.where(finish > t, 1.0, 0.0) for t in range(T)]

    head = lax.broadcasted_iota(jnp.int32, (S, HL), 1)
    lane = lax.broadcasted_iota(jnp.int32, (S, 128), 1)
    spread_row = lax.broadcasted_iota(jnp.int32, (2 * HL, IL), 0)
    spread_col = lax.broadcasted_iota(jnp.int32, (2 * HL, IL), 1)
    spread_from = jnp.where(spread_row >= HL, spread_row - HL, spread_row) * HEAD_DIM
    offset = spread_col - spread_from
    spread = jnp.where((offset >= 0) & (offset < HEAD_DIM), 1.0, 0.0).astype(BF16)

    def convolve(h, ts, seq, bc_seq):
        for t in ts:
            mixed = conv_b_ref[...]
            for k in range(4):
                mixed = mixed + conv_w_ref[k : k + 1, :] * seq[t + k]
            xs[t * S : (t + 1) * S] = silu(mixed)
            mixed = bc_b_ref[:, group_cols]
            for k in range(4):
                mixed = mixed + bc_w_ref[k : k + 1, group_cols] * bc_seq[t + k]
            act = silu(mixed)
            for g in range(NG):
                low = g * 2 * STATE
                row = t - ts[0]
                bs[t, :, g * STATE : (g + 1) * STATE] = act[:, low : low + STATE]
                cs[h, row, :, g * STATE : (g + 1) * STATE] = act[:, low + STATE : low + 2 * STATE]
        for row in range(len(ts), 8):
            cs[h, row] = jnp.zeros((S, NG * STATE), F32)

    def contract(h, count):
        batch = 4 if S % 4 == 0 else 1

        def some_slots(i, _):
            if h == 0:
                for b in range(batch):
                    state_copy(i * batch + b).wait()
            for b in range(batch):
                s = i * batch + b
                rows8 = cs[h, :, s, :]
                for g in range(NG):
                    cg = rows8[:, g * STATE : (g + 1) * STATE]
                    high = cg.astype(BF16).astype(F32)
                    lhs = jnp.concatenate([high, cg - high], axis=0).astype(BF16)
                    held = st[s, g * GH : (g + 1) * GH].reshape(GH * HEAD_DIM, STATE).astype(BF16)
                    both = lax.dot_general(
                        lhs, held, (((1,), (1,)), ((), ())), preferred_element_type=F32
                    )
                    value = both[0:count] + both[8 : 8 + count]
                    y0[0:count, s, g * GH * HEAD_DIM : (g + 1) * GH * HEAD_DIM] = value
            return 0

        lax.fori_loop(0, S // batch, some_slots, 0)

    carry = {"start": None, "weights": []}

    def combine(h, ts, raw_of, gate_of):
        squares = jnp.zeros((S, 128), F32)
        for t in ts:
            row = t - ts[0]
            size = softplus(raw_of(t) + delta_b_ref[...]) * live[t]
            keep = jnp.exp(-size * decay_ref[...])
            carry["start"] = keep if t == 0 else carry["start"] * keep
            carry["weights"] = [w * keep for w in carry["weights"]] + [size]
            blocks = [carry["start"]]
            for u in range(t + 1):
                scores = jnp.zeros((S, HL), F32)
                for g in range(NG):
                    span = slice(g * STATE, (g + 1) * STATE)
                    score = jnp.sum(cs[h, row, :, span] * bs[u, :, span], axis=1, keepdims=True)
                    inside = (head >= g * GH) & (head < (g + 1) * GH)
                    scores = jnp.where(inside, score, scores)
                block = carry["weights"][u] * scores
                if u == t:
                    block = block + skip_ref[...]
                blocks.append(block)
            table = jnp.concatenate(blocks, axis=0)
            high = table.astype(BF16).astype(F32)
            table = jnp.concatenate([high, table - high], axis=1).astype(BF16)
            width = min(IL, 512)
            square = jnp.zeros((S, 1), F32)
            for low in range(0, IL, width):
                cols = slice(low, low + width)
                wide = dot(table, spread[:, cols])
                total = wide[0:S] * y0[row, :, cols]
                for u in range(t + 1):
                    total = total + wide[(u + 1) * S : (u + 2) * S] * xs[u * S : (u + 1) * S, cols]
                gated = total * silu(gate_of(t, cols))
                square = square + jnp.sum(gated * gated, axis=1, keepdims=True)
                hidden[h, row * S : (row + 1) * S, cols] = (gated * gain_ref[:, cols]).astype(BF16)
            squares = jnp.where(lane == t, square, squares)
        sq_mine[h] = squares
        for o in range(TP - 1):
            sq_copy(h, o).start()

    def project(h):
        for o in range(1, TP):
            if h == 0:
                w_copy(o).wait()
            part[h, o - 1] = dot(hidden[h], wv[o]).astype(BF16)
            part_copy(h, o - 1).start()
        if h == 0:
            w_copy(0).wait()
        own_part[h] = dot(hidden[h], wv[0])

    def finish_half(h, ts):
        squares = sq_mine[h]
        for o in range(TP - 1):
            sq_copy(h, o).wait()
            squares = squares + sq_got[h, o]
        inv_rms = lax.rsqrt(squares / INNER + EPS)
        scale = jnp.concatenate([inv_rms[:, t : t + 1] * live[t] for t in ts], axis=0)
        total = own_part[h]
        for o in range(TP - 1):
            part_copy(h, o).wait()
            total = total + part_got[h, o].astype(F32)
        return (total * scale).astype(BF16)

    early, late = list(range(PERIOD)), list(range(PERIOD, T))
    seq = [conv_state_ref[k].astype(F32) for k in range(3)]
    seq += [conv_ref[t].astype(F32) for t in early]
    bc_seq = [bc_state_ref[k, :, group_cols].astype(F32) for k in range(3)]
    bc_seq += [bc_ref[t, :, group_cols].astype(F32) for t in early]
    convolve(0, early, seq, bc_seq)
    contract(0, PERIOD)
    combine(
        0,
        early,
        lambda t: delta_ref[t].astype(F32),
        lambda t, cols: gate_ref[t, :, cols].astype(F32),
    )
    project(0)

    take_a, take_b = unpack_matrix(S, moved, R - 1, serve_take)
    own = 1.0 - named(S, R - 1, serve_take)
    own_rows = jnp.concatenate([own] * moved, axis=0)
    for o in range(R - 1):
        msg_copy(o).wait()
    arrived = got[...].reshape((R - 1) * 16, IL + GC + 128)
    new_gates[...] = dot(take_a, arrived[:, 0:IL]) + own_rows * gate_rows.astype(F32)
    new_conv = dot(take_b, arrived[:, 0:IL]) + own_rows * conv_rows.astype(F32)
    tail = dot(take_a, arrived[:, IL:])
    new_bc = tail[:, 0:GC] + own_rows * bc_rows.astype(F32)
    new_delta = tail[:, GC : GC + HL] + own_rows * delta_rows.astype(F32)
    seq = [conv_ref[t].astype(F32) if t < PERIOD else None for t in range(PERIOD)]
    seq = [None] * 3 + seq + [new_conv[k * S : (k + 1) * S] for k in range(moved)]
    bc_seq = [None] * 3 + [bc_ref[t, :, group_cols].astype(F32) for t in range(PERIOD)]
    bc_seq += [new_bc[k * S : (k + 1) * S] for k in range(moved)]
    convolve(1, late, seq, bc_seq)
    contract(1, moved)
    combine(
        1,
        late,
        lambda t: new_delta[(t - PERIOD) * S : (t - PERIOD + 1) * S],
        lambda t, cols: new_gates[(t - PERIOD) * S : (t - PERIOD + 1) * S, cols],
    )
    project(1)

    out_ref[0:PERIOD] = finish_half(0, early).reshape(PERIOD, S, DL)
    half = DL // 2
    give_a, give_b = pack_matrix(S, moved, R - 1, give_send)
    put_a, put_b = unpack_matrix(S, moved, R - 1, give_take)
    is_target = named(S, R - 1, give_take)
    keep_rows = jnp.concatenate([own * (1.0 - is_target)] * moved, axis=0)

    later = finish_half(1, late)
    packed = dot(give_a, later[:, 0:half]) + dot(give_b, later[:, half:])
    back[...] = packed.astype(BF16).reshape(R - 1, 16, half)

    def back_copy(o):
        return pltpu.make_async_remote_copy(
            src_ref=back.at[o],
            dst_ref=back_got.at[o],
            send_sem=back_send.at[o],
            recv_sem=back_recv.at[o],
            device_id={"rep": ahead(o)},
            device_id_type=MESH,
        )

    for o in range(R - 1):
        back_copy(o).start()
    stay = keep_rows * later.astype(F32)
    for o in range(R - 1):
        back_copy(o).wait()
    arrived = back_got[...].reshape((R - 1) * 16, half)
    left = (dot(put_a, arrived) + stay[:, 0:half]).astype(BF16)
    right = (dot(put_b, arrived) + stay[:, half:]).astype(BF16)
    out_ref[PERIOD:, :, 0:half] = left.reshape(moved, S, half)
    out_ref[PERIOD:, :, half:] = right.reshape(moved, S, half)


def body(R, TP, *arrays):
    (gate, conv, bc, delta, conv_w, conv_b, bc_w, bc_b, delta_b, decay, skip, gain, w, state,
     conv_state, bc_state, finish, plan) = arrays
    T, S, IL = gate.shape
    HL = delta.shape[2]
    NG = max(1, HL * GROUPS // HEADS)
    D = w.shape[1]
    DL = D // TP
    GC = NG * 2 * STATE
    wide = IL + GC + 128
    dims = (T, S, IL, HL, NG, R, TP, DL)
    vmem = pl.BlockSpec(memory_space=pltpu.VMEM)
    hbm = pl.BlockSpec(memory_space=pl.ANY)
    smem = pl.BlockSpec(memory_space=pltpu.SMEM)
    dma = pltpu.SemaphoreType.DMA
    half = DL // 2
    rows = PERIOD * S
    return pl.pallas_call(
        functools.partial(kernel, dims),
        out_shape=jax.ShapeDtypeStruct((T, S, DL), BF16),
        in_specs=[vmem] * 12 + [hbm, hbm] + [vmem] * 2 + [smem] * 2,
        out_specs=vmem,
        scratch_shapes=[
            pltpu.VMEM((S, HL, HEAD_DIM, STATE), F32),
            pltpu.VMEM((TP, IL, DL), BF16),
            pltpu.VMEM((R - 1, 16, wide), BF16),
            pltpu.VMEM((R - 1, 16, wide), BF16),
            pltpu.VMEM((T * S, IL), F32),
            pltpu.VMEM((T, S, NG * STATE), F32),
            pltpu.VMEM((2, 8, S, NG * STATE), F32),
            pltpu.VMEM((rows // S, S, IL), F32),
            pltpu.VMEM((rows, IL), F32),
            pltpu.VMEM((2, rows, IL), BF16),
            pltpu.VMEM((2, S, 128), F32),
            pltpu.VMEM((2, TP - 1, S, 128), F32),
            pltpu.VMEM((2, rows, DL), F32),
            pltpu.VMEM((2, TP - 1, rows, DL), BF16),
            pltpu.VMEM((2, TP - 1, rows, DL), BF16),
            pltpu.VMEM((R - 1, 16, half), BF16),
            pltpu.VMEM((R - 1, 16, half), BF16),
            dma((S,)),
            dma((TP,)),
            dma((R - 1,)),
            dma((R - 1,)),
            dma((2, TP - 1)),
            dma((2, TP - 1)),
            dma((2, TP - 1)),
            dma((2, TP - 1)),
            dma((R - 1,)),
            dma((R - 1,)),
        ],
        compiler_params=pltpu.CompilerParams(
            collective_id=0, has_side_effects=True, vmem_limit_bytes=58 * 1024 * 1024
        ),
    )(
        gate,
        conv,
        bc,
        delta,
        conv_w,
        conv_b.reshape(1, -1),
        bc_w,
        bc_b.reshape(1, -1),
        delta_b.reshape(1, -1),
        decay.reshape(1, -1),
        skip.reshape(1, -1),
        gain.reshape(1, -1),
        w,
        state,
        conv_state.transpose(1, 0, 2),
        bc_state.transpose(1, 0, 2),
        finish,
        plan.transpose(0, 1, 3, 4, 2).reshape(R * CAP, 2, R),
    )


def solution(mesh):
    rows = ("parts", "rep")
    in_specs = (
        P(None, rows, "tp"),
        P(None, rows, "tp"),
        P(None, rows, None),
        P(None, rows, "tp"),
        P(None, "tp"),
        P("tp"),
        P(),
        P(),
        P("tp"),
        P("tp"),
        P("tp"),
        P("tp"),
        P("tp", None),
        P(rows, "tp", None, None),
        P(rows, None, "tp"),
        P(rows, None, None),
        P(rows),
        P("parts", None, None, None, None),
    )
    return jax.shard_map(
        functools.partial(body, mesh.shape["rep"], mesh.shape["tp"]),
        mesh=mesh,
        in_specs=in_specs,
        out_specs=P(None, rows, "tp"),
        check_vma=False,
    )
```

time: 48 us -> 41.2 us (0.86)
  the two profiles are of different devices: /device:TPU:13 before, /device:TPU:0 now
where the time goes in v2:
time: 41.2 us; the launch traced here: 41 us
  Pallas kernels  39.4 us (96%)
  local copies, waits for them, and re-layouts  1.62 us (4%)
    pallas_call x1, Pallas kernels, body(): pl.pallas_call(functools.partial(kernel, dims), out_shape=jax.ShapeDtypeS...  39.4 us
    unnamed x1, local copies, waits for them, and re-layouts  1.62 us

profile of v2, /device:TPU:0, one launch (start us, length us, event | category | flops | bytes accessed | tf_op | source)
XLA Modules:
  0.0 41.0 jit_solution(14752988533285499825)
XLA Ops:
  0.0 39.4 %shard_map.172 = bf16[6,16,1024]{2,1,0:T(8,128)(2,1)} custom-call(bf16[6,16,2048]{2,1,0:T(8,128)(2,1)} %gate_ref.1, bf16[6,16,2048]{2,1,0:T(8,128)(2,1)} %conv_ref.1, bf16[6,16,2048]{2,1,0:T(8,128)(2,1)} %bc_ref.1, bf16[6,16,32]{2,1,0:T(8,128)(2,1)} %delta_ref.1, f32[4,2048]{1,0:T(4,128)} %conv_w_ref.1, f32[1,2048]{1,0:T(1,128)} %bitcast.13, ...), custom_call_target="tpu_custom_call" | custom-call | tf_op jit(solution)/shard_map/pallas_call | solution.py:434
  39.4 1.6 %copy.23 = bf16[6,16,1024]{2,1,0:T(8,128)(2,1)} copy(bf16[6,16,1024]{2,1,0:T(8,128)(2,1)} %shard_map.172) | data formatting | bytes 393216

commit v3 on v2

--- a/solution.py
+++ b/solution.py
@@ -136,11 +136,22 @@
     me = lax.axis_index("rep")
     tp = lax.axis_index("tp")
 
+    stages = TP.bit_length() - 1
+    by_stage = [[m for m in reversed(range(1, TP)) if m & -m == 1 << k] for k in range(stages)]
+
+    def flipped(mask):
+        index = tp
+        for k in range(stages):
+            if mask >> k & 1:
+                bit = lax.rem(tp // (1 << k), 2)
+                index = index + (1 << k) * (1 - 2 * bit)
+        return index
+
     def state_copy(s):
         return pltpu.make_async_copy(state_hbm.at[s], st.at[s], st_sem.at[s])
 
     def w_copy(o):
-        column = pl.multiple_of(lax.rem(tp + o, TP) * DL, DL)
+        column = pl.multiple_of(flipped(o) * DL, DL)
         return pltpu.make_async_copy(w_hbm.at[:, pl.ds(column, DL)], wv.at[o], w_sem.at[o])
 
     barrier = pltpu.get_barrier_semaphore()
@@ -155,8 +166,8 @@
 
     for s in range(S):
         state_copy(s).start()
-    for o in list(range(1, TP)) + [0]:
-        w_copy(o).start()
+    for m in sum(by_stage, []) + [0]:
+        w_copy(m).start()
 
     def entry(source, target, c, which):
         return plan_ref[source * CAP + c, which, target]
@@ -211,13 +222,13 @@
             device_id_type=MESH,
         )
 
-    def part_copy(h, o):
+    def part_copy(h, m):
         return pltpu.make_async_remote_copy(
-            src_ref=part.at[h, o],
-            dst_ref=part_got.at[h, o],
-            send_sem=part_send.at[h, o],
-            recv_sem=part_recv.at[h, o],
-            device_id={"tp": lax.rem(tp + (o + 1), TP)},
+            src_ref=part.at[h, m],
+            dst_ref=part_got.at[h, m],
+            send_sem=part_send.at[h, m],
+            recv_sem=part_recv.at[h, m],
+            device_id={"tp": flipped(m & -m)},
             device_id_type=MESH,
         )
 
@@ -319,14 +330,31 @@
             sq_copy(h, o).start()
 
     def project(h):
-        for o in range(1, TP):
-            if h == 0:
-                w_copy(o).wait()
-            part[h, o - 1] = dot(hidden[h], wv[o]).astype(BF16)
-            part_copy(h, o - 1).start()
+        for k in range(stages):
+            for m in by_stage[k]:
+                if h == 0:
+                    w_copy(m).wait()
+                block = dot(hidden[h], wv[m])
+                if k == 0:
+                    part[h, m] = block.astype(BF16)
+                    part_copy(h, m).start()
+                else:
+                    own_part[h, m] = block
         if h == 0:
             w_copy(0).wait()
-        own_part[h] = dot(hidden[h], wv[0])
+        own_part[h, 0] = dot(hidden[h], wv[0])
+
+    def relay(h):
+        for k in range(1, stages):
+            for m in by_stage[k - 1]:
+                part_copy(h, m).wait()
+                kept = m - (1 << (k - 1))
+                block = own_part[h, kept] + part_got[h, m].astype(F32)
+                if kept in by_stage[k]:
+                    part[h, kept] = block.astype(BF16)
+                    part_copy(h, kept).start()
+                else:
+                    own_part[h, kept] = block
 
     def finish_half(h, ts):
         squares = sq_mine[h]
@@ -335,10 +363,11 @@
             squares = squares + sq_got[h, o]
         inv_rms = lax.rsqrt(squares / INNER + EPS)
         scale = jnp.concatenate([inv_rms[:, t : t + 1] * live[t] for t in ts], axis=0)
-        total = own_part[h]
-        for o in range(TP - 1):
-            part_copy(h, o).wait()
-            total = total + part_got[h, o].astype(F32)
+        total = own_part[h, 0]
+        if stages:
+            last = 1 << (stages - 1)
+            part_copy(h, last).wait()
+            total = total + part_got[h, last].astype(F32)
         return (total * scale).astype(BF16)
 
     early, late = list(range(PERIOD)), list(range(PERIOD, T))
@@ -373,6 +402,7 @@
     bc_seq += [new_bc[k * S : (k + 1) * S] for k in range(moved)]
     convolve(1, late, seq, bc_seq)
     contract(1, moved)
+    relay(0)
     combine(
         1,
         late,
@@ -383,6 +413,7 @@
 
     out_ref[0:PERIOD] = finish_half(0, early).reshape(PERIOD, S, DL)
     half = DL // 2
+    relay(1)
     give_a, give_b = pack_matrix(S, moved, R - 1, give_send)
     put_a, put_b = unpack_matrix(S, moved, R - 1, give_take)
     is_target = named(S, R - 1, give_take)
@@ -449,9 +480,9 @@
             pltpu.VMEM((2, rows, IL), BF16),
             pltpu.VMEM((2, S, 128), F32),
             pltpu.VMEM((2, TP - 1, S, 128), F32),
-            pltpu.VMEM((2, rows, DL), F32),
-            pltpu.VMEM((2, TP - 1, rows, DL), BF16),
-            pltpu.VMEM((2, TP - 1, rows, DL), BF16),
+            pltpu.VMEM((2, TP, rows, DL), F32),
+            pltpu.VMEM((2, TP, rows, DL), BF16),
+            pltpu.VMEM((2, TP, rows, DL), BF16),
             pltpu.VMEM((R - 1, 16, half), BF16),
             pltpu.VMEM((R - 1, 16, half), BF16),
             dma((S,)),
@@ -460,8 +491,8 @@
             dma((R - 1,)),
             dma((2, TP - 1)),
             dma((2, TP - 1)),
-            dma((2, TP - 1)),
-            dma((2, TP - 1)),
+            dma((2, TP)),
+            dma((2, TP)),
             dma((R - 1,)),
             dma((R - 1,)),
         ],

time: 41.2 us -> 42.6 us (1.034)
  Pallas kernels: 39.4 us -> 40.8 us
    pallas_call x1, Pallas kernels: 39.4 us -> 40.8 us  [body(): pl.pallas_call(functools.partial(kernel, dims), out_shape=jax.ShapeDtypeS...]
where the time goes in v3:
time: 42.6 us; the launch traced here: 42.4 us
  Pallas kernels  40.8 us (96%)
  local copies, waits for them, and re-layouts  1.62 us (4%)
    pallas_call x1, Pallas kernels, body(): pl.pallas_call(functools.partial(kernel, dims), out_shape=jax.ShapeDtypeS...  40.8 us
    unnamed x1, local copies, waits for them, and re-layouts  1.62 us

profile of v3, /device:TPU:0, one launch (start us, length us, event | category | flops | bytes accessed | tf_op | source)
XLA Modules:
  0.0 42.4 jit_solution(4925734566469861883)
XLA Ops:
  0.0 40.8 %shard_map.172 = bf16[6,16,1024]{2,1,0:T(8,128)(2,1)} custom-call(bf16[6,16,2048]{2,1,0:T(8,128)(2,1)} %gate_ref.1, bf16[6,16,2048]{2,1,0:T(8,128)(2,1)} %conv_ref.1, bf16[6,16,2048]{2,1,0:T(8,128)(2,1)} %bc_ref.1, bf16[6,16,32]{2,1,0:T(8,128)(2,1)} %delta_ref.1, f32[4,2048]{1,0:T(4,128)} %conv_w_ref.1, f32[1,2048]{1,0:T(1,128)} %bitcast.13, ...), custom_call_target="tpu_custom_call" | custom-call | tf_op jit(solution)/shard_map/pallas_call | solution.py:465
  40.8 1.6 %copy.23 = bf16[6,16,1024]{2,1,0:T(8,128)(2,1)} copy(bf16[6,16,1024]{2,1,0:T(8,128)(2,1)} %shard_map.172) | data formatting | bytes 393216
